TPU v7x, 32 devices: a whole 2x2x4 slice. The times are simulated.
32 devices in a mesh: band: 8 (over y, x, core), grid: 4 (over z).
Axes of the slice: x: 2, y: 2, z: 4, core: 2. Of those that a mesh axis runs over, the one named last changes fastest.
Arguments:
- own_orbitals: bfloat16 [16, 128, 128, 128], P('band', 'grid'), may hold values from -9 to 9
- resident_orbitals: bfloat16 [16, 128, 128, 128], P('band', 'grid'), may hold values from -9 to 9
- pair_lists: int32 [8, 2, 2, 2], P('band'), may hold values from 0 to 1, as said below
- pair_counts: int32 [8, 2], P('band'), may hold values from 1 to 2, as said below
Outputs:
- exchange_block: bfloat16 [16, 128, 128, 128], P('band', 'grid')
- intersection: float32 [16, 2], P('band')
Inputs may be any that keep to these rules, and one draw needn't show every extreme that they name: pair_lists[b, l, s] = (i, j) pairs band i of block b with band j of the partner block of list l; the 2 pairs of one list are distinct; slots s >= pair_counts[b, l] hold pairs that are not used. `pair_counts`: in each of the two lists exactly one block has 2 live slots, every other block exactly 1.
All inputs are finite; a program needn't handle non-finite values.
Results may differ from a plain program's by a relative error of at most 0.00045.
Values may be sent and summed in bfloat16 or wider, within the bound.
A program may use at most 64 MiB of HBM per device.

v0:
```python
import functools
import math

import jax
import jax.numpy as jnp
import numpy as np
import ml_dtypes
from jax import lax
from jax.experimental import pallas as pl
from jax.experimental.pallas import tpu as pltpu
from jax.sharding import PartitionSpec as P

F32 = jnp.float32
BF16 = jnp.bfloat16
I16 = jnp.int16
MESH = pl.DeviceIdType.MESH
FINE_ROWS = 16
FINE = 65000.0
TOP = 32700.0
LIMIT = 56 * 2**20


def tables(length, parts):
    k = np.arange(length)
    angles = (np.outer(k, k) % length) * (2.0 * math.pi / length)
    cas = (np.cos(angles) + np.sin(angles)) / math.sqrt(length)
    order = sorted(range(length), key=lambda i: (min(i, length - i), i))
    rows = length // parts
    perm = np.array([order[r * parts + g] for g in range(parts) for r in range(rows)])

    def split(m):
        high = m.astype(np.float32).astype(ml_dtypes.bfloat16)
        low = (m - high.astype(np.float64)).astype(np.float32).astype(ml_dtypes.bfloat16)
        return high, low

    def left(m):
        high, low = split(m)
        return np.block([[high, high], [low, np.zeros_like(low)]])

    def right(m):
        high, low = split(m)
        return np.block([[high, low], [high, np.zeros_like(low)]])

    return [
        jnp.asarray(t.astype(ml_dtypes.bfloat16))
        for t in (right(cas), left(cas[perm, :]), left(cas), left(cas[:, perm]))
    ]


def halves(v):
    high = v.astype(BF16)
    return high, (v - high.astype(F32)).astype(BF16)


def times_right(v, table):
    high, low = halves(v)
    n = v.shape[1]
    out = jnp.dot(jnp.concatenate([high, low], 1), table, preferred_element_type=F32)
    return out[:, :n] + out[:, n:]


def times_left(table, a, b):
    ah, al = halves(a)
    bh, bl = halves(b)
    rhs = jnp.concatenate(
        [jnp.concatenate([ah, bh], 1), jnp.concatenate([al, bl], 1)], 0
    )
    out = jnp.dot(table, rhs, preferred_element_type=F32)
    n = a.shape[0]
    return out[:n] + out[n:]


def tile_max(running, v):
    return jnp.maximum(running, jnp.max(jnp.abs(v).reshape(-1, 8, v.shape[-1]), axis=0))


def folded(index, length):
    return jnp.minimum(index, length - index)


def code_of(peak):
    peak = jnp.maximum(jnp.max(peak, keepdims=True), 1e-30)
    return jnp.ceil(jnp.log2(peak) * 256.0)


def size_of(code):
    return jnp.exp2(code * (1.0 / 256.0))


class Sizes:
    def __init__(self, bands, planes, length):
        self.bands = bands
        self.planes = planes
        self.length = length
        self.parts = length // planes
        self.rows = planes
        self.fine = max(2, FINE_ROWS // self.parts)
        self.all_rows = self.rows + self.fine + 1
        self.group = min(8, self.rows)

    def coded(self):
        return (self.parts, self.all_rows, self.planes, self.length)


def write_words(sz, out, where, base, load, inverse, code):
    def words(v):
        return v.astype(jnp.int32).astype(I16)

    def body(r, _):
        out[where, r] = words(jnp.round(load(r) * inverse))
        return 0

    for r in range(sz.fine):
        scaled = load(r) * inverse
        whole = jnp.round(scaled)
        out[where, r] = words(whole)
        out[where, sz.rows + r] = words(jnp.round((scaled - whole) * FINE))
    lax.fori_loop(sz.fine, sz.rows, body, 0, unroll=2)
    out[where, sz.rows + sz.fine] = words(
        jnp.broadcast_to(code, (sz.planes, sz.length))
    )


def forward(sz, own, partner, wz, wy, t):
    n = sz.length

    def body(step, peak):
        x = step * 4
        d = own(x, 4).astype(F32) * partner(x, 4).astype(F32)
        e = times_right(d.reshape(4 * n, n), wz[...])
        for h in range(2):
            a, b = 2 * h, 2 * h + 1
            f = times_left(wy[...], e[a * n : (a + 1) * n], e[b * n : (b + 1) * n])
            t[pl.ds(x + a, n, stride=sz.planes), :] = f[:, :n]
            t[pl.ds(x + b, n, stride=sz.planes), :] = f[:, n:]
            peak = tile_max(peak, f)
        return peak

    return lax.fori_loop(0, sz.planes // 4, body, jnp.zeros((8, 2 * n), F32))


def forward_words(sz, t, out, where, code):
    inverse = TOP / size_of(code)
    base = where * (sz.rows * sz.planes)

    def load(r):
        start = pl.multiple_of(base + r * sz.planes, sz.planes)
        return t[pl.ds(start, sz.planes), :]

    write_words(sz, out, where, base, load, inverse, code)


def set_scales(sz, coded, scales):
    for src in range(sz.parts):
        row = coded[src, sz.rows + sz.fine].astype(jnp.int32).astype(F32)
        scales[src * sz.planes : (src + 1) * sz.planes, :] = size_of(row) * (1.0 / TOP)


def numbers(sz, coded, src, r, is_fine):
    v = coded[src, r].astype(jnp.int32).astype(F32)
    if is_fine:
        v = v + coded[src, sz.rows + r].astype(jnp.int32).astype(F32) * (1.0 / FINE)
    return v


def row_frequency(sz, part, r):
    return ((r * sz.parts + part + 1) // 2).astype(F32)


def column_power(sz, my, power):
    kz = folded(lax.broadcasted_iota(jnp.int32, (8, sz.length), 1), sz.length).astype(F32)
    squared = jnp.maximum(kz * kz + my * my, 1.0)
    root = jnp.sqrt(squared)
    w = root * jnp.sqrt(root)
    return (w if power > 0 else 1.0 / w)[0:1]


def middle(sz, me, coded, wx, scales, u):
    n = sz.length
    set_scales(sz, coded, scales)
    factor = 0.25 * n**1.5

    def squares():
        kx = folded(lax.broadcasted_iota(jnp.int32, (n, n), 0), n)
        kz = folded(lax.broadcasted_iota(jnp.int32, (n, n), 1), n)
        return (kx * kx + kz * kz).astype(F32)

    def pair(r, is_fine, peak):
        g = [
            jnp.concatenate(
                [numbers(sz, coded, src, r + h, is_fine) for src in range(sz.parts)], 0
            )
            * scales[...]
            for h in range(2)
        ]
        s = times_left(wx[...], g[0], g[1])
        base = squares()
        filtered = []
        my = [row_frequency(sz, me, jnp.int32(r) + h) for h in range(2)]
        for h in range(2):
            k = base + my[h] * my[h]
            k = jnp.where(k > 0.5, factor / jnp.maximum(k, 1.0), 0.0)
            filtered.append(s[:, h * n : (h + 1) * n] * k)
        back = times_left(wx[...], filtered[0], filtered[1])
        for h in range(2):
            v = back[:, h * n : (h + 1) * n] * column_power(sz, my[h], 1)
            u[r + h] = v
            peak = tile_max(peak, v)
        return peak

    peak = jnp.zeros((8, n), F32)
    for r in range(0, sz.fine, 2):
        peak = pair(r, True, peak)
    return lax.fori_loop(
        sz.fine // 2, sz.rows // 2, lambda s, p: pair(s * 2, False, p), peak
    )


def middle_words(sz, u, out, where, code):
    inverse = TOP / size_of(code)

    def load(r):
        return u[r, pl.ds(pl.multiple_of(where * sz.planes, sz.planes), sz.planes), :]

    write_words(sz, out, where, None, load, inverse, code)


def backward(sz, coded, wz, wyi, scales, t, partner, add):
    n = sz.length
    set_scales(sz, coded, scales)
    for src in range(sz.parts):

        def put(r, is_fine):
            my = row_frequency(sz, src, jnp.int32(r))
            scale = scales[src * sz.planes : src * sz.planes + 8, :][0:1]
            v = numbers(sz, coded, src, r, is_fine) * (scale * column_power(sz, my, -1))
            start = pl.multiple_of((src * sz.rows + r) * sz.planes, sz.planes)
            t[pl.ds(start, sz.planes), :] = v

        for r in range(sz.fine):
            put(r, True)

        def body(r, _):
            put(r, False)
            return 0

        lax.fori_loop(sz.fine, sz.rows, body, 0, unroll=2)

    def planes(step, _):
        x = step * 2
        a = t[pl.ds(x, n, stride=sz.planes), :]
        b = t[pl.ds(x + 1, n, stride=sz.planes), :]
        f = times_left(wyi[...], a, b)
        v = times_right(jnp.concatenate([f[:, :n], f[:, n:]], 0), wz[...])
        add(x, v.reshape(2, n, n) * partner(x, 2).astype(F32))
        return 0

    lax.fori_loop(0, sz.planes // 2, planes, 0, unroll=2)


def regular_kernel(
    sz, lists, own, resident, wz, wy, wx, wyi, total, received,
    arrived, t, u, scales, out1, in1, out2, in2,
    send_sem, recv_sem, pass_send, pass_recv, local_sem, save_sem,
):
    me = lax.axis_index("grid")
    block = lax.axis_index("band")
    blocks = lax.axis_size("band")
    parts = sz.parts
    after = lax.rem(block + 1, blocks)
    before = lax.rem(block + blocks - 1, blocks)

    barrier = pltpu.get_barrier_semaphore()
    for o in range(1, parts):
        pl.semaphore_signal(
            barrier, inc=1, device_id=(block, lax.rem(me + o, parts)), device_id_type=MESH
        )
    for other in (after, before):
        pl.semaphore_signal(barrier, inc=1, device_id=(other, me), device_id_type=MESH)
    pl.semaphore_wait(barrier, parts + 1)

    passing = pltpu.make_async_remote_copy(
        src_ref=resident, dst_ref=arrived, send_sem=pass_send, recv_sem=pass_recv,
        device_id=(after, me), device_id_type=MESH,
    )
    passing.start()

    firsts = [lists[0, l, 0, 0] for l in range(2)]
    seconds = [lists[0, l, 0, 1] for l in range(2)]
    partners = (resident, arrived)

    def remote(phase, src, dst, l, o):
        to = lax.rem(me + o, parts)
        return pltpu.make_async_remote_copy(
            src_ref=src.at[l, to], dst_ref=dst.at[l, me],
            send_sem=send_sem.at[phase, l, o], recv_sem=recv_sem.at[phase, l, o],
            device_id=(block, to), device_id_type=MESH,
        )

    def send(phase, src, dst, l, write):
        copies = []
        for o in range(1, parts):
            write(lax.rem(me + o, parts))
            c = remote(phase, src, dst, l, o)
            c.start()
            copies.append(c)
        write(me)
        c = pltpu.make_async_copy(src.at[l, me], dst.at[l, me], local_sem.at[phase, l])
        c.start()
        copies.append(c)
        return copies

    flights = {}
    for l in range(2):
        if l == 1:
            passing.wait()
            saving = pltpu.make_async_copy(arrived, received, save_sem)
            saving.start()
        peak = forward(
            sz,
            lambda x, c: own[firsts[l], pl.ds(x, c)],
            lambda x, c: partners[l][seconds[l], pl.ds(x, c)],
            wz, wy, t,
        )
        code = code_of(peak)
        flights[0, l] = send(
            0, out1, in1, l, lambda w: forward_words(sz, t, out1.at[l], w, code)
        )
    for l in range(2):
        for c in flights[0, l]:
            c.wait()
        code = code_of(middle(sz, me, in1.at[l], wx, scales, u))
        flights[1, l] = send(
            1, out2, in2, l, lambda w: middle_words(sz, u, out2.at[l], w, code)
        )
    for l in range(2):
        for c in flights[1, l]:
            c.wait()

        def add(x, v):
            for band in range(sz.bands):
                share = v * (firsts[l] == band).astype(F32)
                if l == 0:
                    total[band, pl.ds(x, 2)] = share
                else:
                    total[band, pl.ds(x, 2)] += share

        backward(
            sz, in2.at[l], wz, wyi, scales, t,
            lambda x, c: partners[l][seconds[l], pl.ds(x, c)], add,
        )
    saving.wait()


def regular(sz, lists, own, resident, wz, wy, wx, wyi):
    n = sz.length
    vmem = pl.BlockSpec(memory_space=pltpu.VMEM)
    coded = pltpu.VMEM((2,) + sz.coded(), I16)
    return pl.pallas_call(
        functools.partial(regular_kernel, sz),
        out_shape=(
            jax.ShapeDtypeStruct(own.shape, F32),
            jax.ShapeDtypeStruct(own.shape, BF16),
        ),
        in_specs=[pl.BlockSpec(memory_space=pltpu.SMEM)] + [vmem] * 6,
        out_specs=(vmem, pl.BlockSpec(memory_space=pl.ANY)),
        scratch_shapes=[
            pltpu.VMEM(own.shape, BF16),
            pltpu.VMEM((n * sz.planes, n), F32),
            pltpu.VMEM((sz.rows, n, n), F32),
            pltpu.VMEM((n, n), F32),
            coded, coded, coded, coded,
            pltpu.SemaphoreType.DMA((2, 2, sz.parts)),
            pltpu.SemaphoreType.DMA((2, 2, sz.parts)),
            pltpu.SemaphoreType.DMA,
            pltpu.SemaphoreType.DMA,
            pltpu.SemaphoreType.DMA((2, 2)),
            pltpu.SemaphoreType.DMA,
        ],
        compiler_params=pltpu.CompilerParams(
            collective_id=0, has_side_effects=True, vmem_limit_bytes=LIMIT
        ),
        name="regular_pairs",
    )(lists, own, resident, wz, wy, wx, wyi)


def extra_forward(sz, own, partner, wz, wy):
    def kernel(own_ref, partner_ref, wz_ref, wy_ref, out, t):
        peak = forward(
            sz, lambda x, c: own_ref[pl.ds(x, c)], lambda x, c: partner_ref[pl.ds(x, c)],
            wz_ref, wy_ref, t,
        )
        code = code_of(peak)
        for g in range(sz.parts):
            forward_words(sz, t, out, g, code)

    return pl.pallas_call(
        kernel,
        out_shape=jax.ShapeDtypeStruct(sz.coded(), I16),
        scratch_shapes=[pltpu.VMEM((sz.length * sz.planes, sz.length), F32)],
        compiler_params=pltpu.CompilerParams(vmem_limit_bytes=LIMIT),
        name="extra_forward",
    )(own, partner, wz, wy)


def extra_middle(sz, coded, wx):
    n = sz.length

    def kernel(coded_ref, wx_ref, out, scales, u):
        me = lax.axis_index("grid")
        code = code_of(middle(sz, me, coded_ref, wx_ref, scales, u))
        for g in range(sz.parts):
            middle_words(sz, u, out, g, code)

    return pl.pallas_call(
        kernel,
        out_shape=jax.ShapeDtypeStruct(sz.coded(), I16),
        scratch_shapes=[pltpu.VMEM((n, n), F32), pltpu.VMEM((sz.rows, n, n), F32)],
        compiler_params=pltpu.CompilerParams(vmem_limit_bytes=LIMIT),
        name="extra_middle",
    )(coded, wx)


def extra_backward(sz, coded, partner, wz, wyi):
    n = sz.length

    def kernel(coded_ref, partner_ref, wz_ref, wyi_ref, out, scales, t):
        def add(x, v):
            out[pl.ds(x, 2)] = v

        backward(
            sz, coded_ref, wz_ref, wyi_ref, scales, t,
            lambda x, c: partner_ref[pl.ds(x, c)], add,
        )

    return pl.pallas_call(
        kernel,
        out_shape=jax.ShapeDtypeStruct((sz.planes, n, n), F32),
        scratch_shapes=[pltpu.VMEM((n, n), F32), pltpu.VMEM((n * sz.planes, n), F32)],
        compiler_params=pltpu.CompilerParams(vmem_limit_bytes=LIMIT),
        name="extra_backward",
    )(coded, partner, wz, wyi)


def finish(sz, own, total):
    def kernel(own_ref, total_ref, out, products):
        t = pl.program_id(0)

        @pl.when(t == 0)
        def _():
            products[...] = jnp.zeros_like(products)

        out[...] = total_ref[...].astype(BF16)
        for i in range(sz.bands):
            for k in range(sz.bands):
                v = own_ref[i].astype(F32) * total_ref[k]
                products[i, k] += jnp.sum(v.reshape(-1, 8, sz.length), axis=0)

    step = 4
    spec = pl.BlockSpec(
        (sz.bands, step, sz.length, sz.length), lambda t: (0, t, 0, 0)
    )
    shape = (sz.bands, sz.bands, 8, sz.length)
    return pl.pallas_call(
        kernel,
        grid=(sz.planes // step,),
        in_specs=[spec, spec],
        out_specs=(spec, pl.BlockSpec(shape, lambda t: (0, 0, 0, 0))),
        out_shape=(
            jax.ShapeDtypeStruct(own.shape, BF16),
            jax.ShapeDtypeStruct(shape, F32),
        ),
        compiler_params=pltpu.CompilerParams(vmem_limit_bytes=LIMIT),
        name="finish",
    )(own, total)


def on_device(own, resident, pair_lists, pair_counts):
    bands, planes, length, _ = own.shape
    sz = Sizes(bands, planes, length)
    wz, wy, wx, wyi = tables(length, sz.parts)
    total, received = regular(sz, pair_lists, own, resident, wz, wy, wx, wyi)
    extras = pair_counts[0] - 1

    def one_pair(step, running):
        l = (step >= extras[0]).astype(jnp.int32)
        slot = 1 + step - l * extras[0]
        row = pair_lists[0, l, slot]
        own_band = lax.dynamic_index_in_dim(own, row[0], 0, keepdims=False)
        partner = jnp.where(
            l == 0,
            lax.dynamic_index_in_dim(resident, row[1], 0, keepdims=False),
            lax.dynamic_index_in_dim(received, row[1], 0, keepdims=False),
        )
        coded = extra_forward(sz, own_band, partner, wz, wy)
        coded = lax.all_to_all(coded, "grid", split_axis=0, concat_axis=0, tiled=True)
        coded = extra_middle(sz, coded, wx)
        coded = lax.all_to_all(coded, "grid", split_axis=0, concat_axis=0, tiled=True)
        term = extra_backward(sz, coded, partner, wz, wyi)
        old = lax.dynamic_index_in_dim(running, row[0], 0, keepdims=False)
        return lax.dynamic_update_index_in_dim(running, old + term, row[0], 0)

    total = lax.fori_loop(0, extras[0] + extras[1], one_pair, total)
    rounded, products = finish(sz, own, total)
    return rounded, lax.psum(jnp.sum(products, axis=(2, 3)), "grid")


def solution(mesh):
    in_specs = (
        P("band", "grid", None, None),
        P("band", "grid", None, None),
        P("band", None, None, None),
        P("band", None),
    )
    out_specs = (P("band", "grid", None, None), P("band", None))
    return jax.shard_map(
        on_device, mesh=mesh, in_specs=in_specs, out_specs=out_specs, check_vma=False
    )
```

profile of v0, /device:TPU:6, one launch (start us, length us, event | category | flops | bytes accessed | tf_op | source)
XLA Modules:
  0.0 228.8 jit_solution(15583714424153976163)
XLA Ops:
  0.6 0.7 fusion
  1.3 0.6 fusion.2
  3.1 0.0 copy-start.3
  3.2 0.0 copy-start.4
  3.2 0.0 copy-start.6
  3.2 118.6 %regular_pairs.1 = (f32[2,32,128,128]{3,2,1,0:T(8,128)}, bf16[2,32,128,128]{3,2,1,0:T(8,128)(2,1)}) custom-call(s32[1,2,2,2]{3,2,1,0:T(2,128)} %lists.1, bf16[2,32,128,128]{3,2,1,0:T(8,128)(2,1)} %own_ref.1, bf16[2,32,128,128]{3,2,1,0:T(8,128)(2,1)} %resident.1, bf16[256,256]{1,0:T(8,128)(2,1)} %constant.38.clone.wz, bf16[256,256]{1,0:T(8,128)(2,1)} %constant.39.clone.wy, ...), custom_call_target="tpu_custom_call" | custom-call | tf_op jit(solution)/shard_map/regular_pairs/pallas_call | solution.py:359
  121.8 0.0 copy-done.3
  121.8 0.0 copy-done.4
  121.8 0.0 copy-done.6
  121.8 88.8 %while.11 = (s32[]{:T(128)}, f32[2,32,128,128]{3,2,1,0:T(8,128)}, s32[]{:T(128)}, s32[2]{0:T(128)S(1)}, s32[1,2,2,2]{3,2,1,0:T(2,128)}, /*index=5*/bf16[2,32,128...) while((s32[]{:T(128)}, f32[2,32,128,128]{3,2,1,0:T(8,128)}, ...), condition=%wide.region_1.2_spmd.clone, body=%wide.region_0.1_spmd.sunk.clone.sunk | while | flops 1048595 | bytes 61243956 | solution.py:503
  121.9 0.7 constant_dynamic-slice_fusion.4
  122.6 0.6 fusion.4
  127.1 3.4 %select_bitcast_fusion.2 = (bf16[32,128,128]{2,1,0:T(8,128)(2,1)}, bf16[32,128,128]{2,1,0:T(8,128)(2,1)}) fusion(bf16[2,32,128,128]{3,2,1,0:T(8,128)(2,1)} %get-tuple-element.227, s32[]{:T(128)S(6)} %select_n.55, bf16[2,32,128,128]{3,2,1,0:T(8,128)(2,1)} %get-tuple-element.226, pred[]{:T(512)S(6)} %eq.6, ...), kind=kLoop, calls=%fused_computation.2.clone.1 | loop fusion | flops 524288 | bytes 5242889 | tf_op jit(solution)/shard_map/while/body/jit(_where)/select_n | solution.py:490
  130.5 7.8 %extra_forward.1 = s16[4,37,32,128]{3,2,1,0:T(8,128)(2,1)} custom-call(bf16[32,128,128]{2,1,0:T(8,128)(2,1)} %get-tuple-element.188.own_ref, bf16[32,128,128]{2,1,0:T(8,128)(2,1)} %get-tuple-element.189.partner_ref, bf16[256,256]{1,0:T(8,128)(2,1)S(1)} %get-tuple-element.231.wz_ref, bf16[256,256]{1,0:T(8,128)(2,1)S(1)} %get-tuple-element.232.wy_ref), custom_call_target="tpu_custom_call" | custom-call | tf_op jit(solution)/shard_map/while/body/extra_forward/pallas_call | solution.py:397
  138.3 27.3 %all_to_all.16.coded_ref = s16[4,37,32,128]{3,2,1,0:T(8,128)(2,1)} all-to-all(s16[4,37,32,128]{3,2,1,0:T(8,128)(2,1)} %extra_forward.1), channel_id=1, replica_groups=mesh['band'=8,'grid'=4] {'grid'}, dimensions={0} | all-to-all | bytes 2424832 | tf_op jit(solution)/shard_map/while/body/all_to_all | solution.py:496
  165.6 9.4 %extra_middle.1 = s16[4,37,32,128]{3,2,1,0:T(8,128)(2,1)} custom-call(s16[4,37,32,128]{3,2,1,0:T(8,128)(2,1)} %all_to_all.16.coded_ref, bf16[256,256]{1,0:T(8,128)(2,1)S(1)} %get-tuple-element.233.wx_ref), custom_call_target="tpu_custom_call" | custom-call | tf_op jit(solution)/shard_map/while/body/extra_middle/pallas_call | solution.py:415
  175.1 3.5 %all-to-all-start.1 = ((s16[4,37,32,128]{3,2,1,0:T(8,128)(2,1)}), s16[4,37,32,128]{3,2,1,0:T(8,128)(2,1)S(1)}, u32[]{:S(2)}, u32[]{:S(2)}) async-start(s16[4,37,32,128]{3,2,1,0:T(8,128)(2,1)} %extra_middle.1), calls=%async_computation.1 | async-start | bytes 2424832 | tf_op jit(solution)/shard_map/while/body/all_to_all | solution.py:498
  178.6 1.7 constant_dynamic-slice_fusion.5
  180.3 15.9 %all-to-all-done.1.coded_ref = s16[4,37,32,128]{3,2,1,0:T(8,128)(2,1)S(1)} async-done(((s16[4,37,32,128]{3,2,1,0:T(8,128)(2,1)}), s16[4,37,32,128]{3,2,1,0:T(8,128)(2,1)S(1)}, u32[]{:S(2)}, u32[]{:S(2)}) %all-to-all-start.1) | async-done | bytes 1212448 | tf_op jit(solution)/shard_map/while/body/all_to_all | solution.py:498
  196.2 0.0 copy-start
  196.2 1.0 copy-done
  197.2 0.0 copy-start.1
  197.3 9.5 %extra_backward.1 = f32[32,128,128]{2,1,0:T(8,128)} custom-call(s16[4,37,32,128]{3,2,1,0:T(8,128)(2,1)} %copy-done, bf16[32,128,128]{2,1,0:T(8,128)(2,1)} %get-tuple-element.189.partner_ref, bf16[256,256]{1,0:T(8,128)(2,1)S(1)} %get-tuple-element.231.wz_ref, bf16[256,256]{1,0:T(8,128)(2,1)} %get-tuple-element.234.wyi_ref), custom_call_target="tpu_custom_call" | custom-call | tf_op jit(solution)/shard_map/while/body/extra_backward/pallas_call | solution.py:436
  206.7 0.0 copy-done.1
  206.7 0.0 copy-start.5
  206.7 0.0 copy-start.7
  206.7 1.9 bitcast_dynamic-update-slice_fusion.2
  208.7 0.0 copy-start.2
  208.7 1.9 copy-done.2
  210.6 0.0 copy-done.5
  210.6 0.0 copy-done.7
  210.6 7.0 %finish.1 = (bf16[2,32,128,128]{3,2,1,0:T(8,128)(2,1)}, f32[2,2,8,128]{3,2,1,0:T(8,128)}) custom-call(bf16[2,32,128,128]{3,2,1,0:T(8,128)(2,1)} %own_ref.1, f32[2,32,128,128]{3,2,1,0:T(8,128)} %get-tuple-element.255), custom_call_target="tpu_custom_call" | custom-call | tf_op jit(solution)/shard_map/finish/pallas_call | solution.py:464
  217.6 0.8 reduce_sum.9
  218.4 10.4 %psum.7 = f32[2,2]{1,0:T(2,128)} all-reduce(f32[2,2]{1,0:T(2,128)S(1)} %reduce_sum.9), channel_id=1, replica_groups=mesh['band'=8,'grid'=4] {'grid'}, use_global_device_ids=true, to_apply=%region_3.4 | all-reduce | flops 4 | bytes 32 | tf_op jit(solution)/shard_map/psum | solution.py:505
Async XLA Ops:
  3.1 118.7 %copy-start.3 = (bf16[256,256]{1,0:T(8,128)(2,1)S(1)}, bf16[256,256]{1,0:T(8,128)(2,1)}, u32[]{:S(2)}) copy-start(bf16[256,256]{1,0:T(8,128)(2,1)} %constant.38.clone.wz) | copy-start | bytes 393220
  3.2 118.7 %copy-start.4 = (bf16[256,256]{1,0:T(8,128)(2,1)S(1)}, bf16[256,256]{1,0:T(8,128)(2,1)}, u32[]{:S(2)}) copy-start(bf16[256,256]{1,0:T(8,128)(2,1)} %constant.39.clone.wy) | copy-start | bytes 393220
  3.2 118.7 %copy-start.6 = (bf16[256,256]{1,0:T(8,128)(2,1)S(1)}, bf16[256,256]{1,0:T(8,128)(2,1)}, u32[]{:S(2)}) copy-start(bf16[256,256]{1,0:T(8,128)(2,1)} %constant.40.clone.wx) | copy-start | bytes 393220
  175.1 21.2 %all-to-all-start.1 = ((s16[4,37,32,128]{3,2,1,0:T(8,128)(2,1)}), s16[4,37,32,128]{3,2,1,0:T(8,128)(2,1)S(1)}, u32[]{:S(2)}, u32[]{:S(2)}) async-start(s16[4,37,32,128]{3,2,1,0:T(8,128)(2,1)} %extra_middle.1), calls=%async_computation.1 | async-start | bytes 2424832 | tf_op jit(solution)/shard_map/while/body/all_to_all | solution.py:498
  196.2 1.0 copy-start
  197.2 9.5 %copy-start.1 = (f32[2,32,128,128]{3,2,1,0:T(8,128)S(1)}, f32[2,32,128,128]{3,2,1,0:T(8,128)}, u32[]{:S(2)}) copy-start(f32[2,32,128,128]{3,2,1,0:T(8,128)} %get-tuple-element.206) | copy-start | bytes 12582916 | tf_op jit(solution)/shard_map/while
  206.7 3.9 %copy-start.5 = (bf16[256,256]{1,0:T(8,128)(2,1)S(1)}, bf16[256,256]{1,0:T(8,128)(2,1)}, u32[]{:S(2)}) copy-start(bf16[256,256]{1,0:T(8,128)(2,1)} %get-tuple-element.253) | copy-start | bytes 393220 | tf_op jit(solution)/shard_map/while
  206.7 3.9 %copy-start.7 = (bf16[256,256]{1,0:T(8,128)(2,1)S(1)}, bf16[256,256]{1,0:T(8,128)(2,1)}, u32[]{:S(2)}) copy-start(bf16[256,256]{1,0:T(8,128)(2,1)} %get-tuple-element.270) | copy-start | bytes 393220 | tf_op jit(solution)/shard_map/while
  208.7 2.0 copy-start.2
where the time goes:
time: 229 us
  Pallas kernels  152 us (66%)
  blocking collectives  37.6 us (16%)
  waiting for transfers between devices  15.9 us (7%)
  other arithmetic  6.87 us (3%)
  local copies, waits for them, and re-layouts  6.61 us (3%)
  loops' own time  4.02 us (2%)
  starting transfers between devices  3.53 us (2%)
    pallas_call x1, Pallas kernels, regular(): pl.pallas_call(functools.partial(regular_kernel, sz), out_shape=(jax.Shap...  119 us
    all_to_all x1, blocking collectives, one_pair(): lax.all_to_all(coded, 'grid', split_axis=0, concat_axis=0, tiled=True)  27.3 us
    all_to_all x1, waiting for transfers between devices, one_pair(): lax.all_to_all(coded, 'grid', split_axis=0, concat_axis=0, tiled=True)  15.9 us
    psum x1, blocking collectives, on_device(): return (rounded, lax.psum(jnp.sum(products, axis=(2, 3)), 'grid'))  10.4 us
    pallas_call x1, Pallas kernels, extra_backward(): pl.pallas_call(kernel, out_shape=jax.ShapeDtypeStruct((sz.planes, n, n),...  9.46 us
    pallas_call x1, Pallas kernels, extra_middle(): pl.pallas_call(kernel, out_shape=jax.ShapeDtypeStruct(sz.coded(), I16), s...  9.43 us
    pallas_call x1, Pallas kernels, extra_forward(): pl.pallas_call(kernel, out_shape=jax.ShapeDtypeStruct(sz.coded(), I16), s...  7.81 us
    pallas_call x1, Pallas kernels, finish(): pl.pallas_call(kernel, grid=(sz.planes // step,), in_specs=[spec, spec],...  6.99 us
  transfers between devices with their start and end apart: 1, of which 1 were waited for; matrix products, arithmetic and copies ran while one was open for 1% of the time, Pallas kernels for 0%

commit v1 on v0

--- a/solution.py
+++ b/solution.py
@@ -14,7 +14,7 @@
 BF16 = jnp.bfloat16
 I16 = jnp.int16
 MESH = pl.DeviceIdType.MESH
-FINE_ROWS = 16
+FINE_ROWS = 8
 FINE = 65000.0
 TOP = 32700.0
 LIMIT = 56 * 2**20
@@ -225,7 +225,7 @@
     write_words(sz, out, where, None, load, inverse, code)
 
 
-def backward(sz, coded, wz, wyi, scales, t, partner, add):
+def backward(sz, coded, wz, wyi, scales, t, partner, add, start=0):
     n = sz.length
     set_scales(sz, coded, scales)
     for src in range(sz.parts):
@@ -234,8 +234,8 @@
             my = row_frequency(sz, src, jnp.int32(r))
             scale = scales[src * sz.planes : src * sz.planes + 8, :][0:1]
             v = numbers(sz, coded, src, r, is_fine) * (scale * column_power(sz, my, -1))
-            start = pl.multiple_of((src * sz.rows + r) * sz.planes, sz.planes)
-            t[pl.ds(start, sz.planes), :] = v
+            first = pl.multiple_of((src * sz.rows + r) * sz.planes, sz.planes)
+            t[pl.ds(first, sz.planes), :] = v
 
         for r in range(sz.fine):
             put(r, True)
@@ -246,22 +246,21 @@
 
         lax.fori_loop(sz.fine, sz.rows, body, 0, unroll=2)
 
-    def planes(step, _):
+    def planes(step, carried):
         x = step * 2
         a = t[pl.ds(x, n, stride=sz.planes), :]
         b = t[pl.ds(x + 1, n, stride=sz.planes), :]
         f = times_left(wyi[...], a, b)
         v = times_right(jnp.concatenate([f[:, :n], f[:, n:]], 0), wz[...])
-        add(x, v.reshape(2, n, n) * partner(x, 2).astype(F32))
-        return 0
-
-    lax.fori_loop(0, sz.planes // 2, planes, 0, unroll=2)
-
-
-def regular_kernel(
-    sz, lists, own, resident, wz, wy, wx, wyi, total, received,
-    arrived, t, u, scales, out1, in1, out2, in2,
-    send_sem, recv_sem, pass_send, pass_recv, local_sem, save_sem,
+        return add(x, v.reshape(2, n, n) * partner(x, 2).astype(F32), carried)
+
+    return lax.fori_loop(0, sz.planes // 2, planes, start, unroll=2)
+
+
+def pairs_kernel(
+    sz, lists, counts, own, resident, early, wz, wy, wx, wyi, result, inner,
+    total, arrived, t, u, scales, out1, in1, out2, in2, terms,
+    send_sem, recv_sem, pass_send, pass_recv, local_sem, term_send, term_recv,
 ):
     me = lax.axis_index("grid")
     block = lax.axis_index("band")
@@ -285,23 +284,38 @@
     )
     passing.start()
 
+    more = [counts[0, l] > 1 for l in range(2)]
+    both = more[0] & more[1]
     firsts = [lists[0, l, 0, 0] for l in range(2)]
     seconds = [lists[0, l, 0, 1] for l in range(2)]
-    partners = (resident, arrived)
-
-    def remote(phase, src, dst, l, o):
-        to = lax.rem(me + o, parts)
-        return pltpu.make_async_remote_copy(
-            src_ref=src.at[l, to], dst_ref=dst.at[l, me],
-            send_sem=send_sem.at[phase, l, o], recv_sem=recv_sem.at[phase, l, o],
-            device_id=(block, to), device_id_type=MESH,
-        )
+    firsts.append(jnp.where(more[1], lists[0, 1, 1, 0], lists[0, 0, 1, 0]))
+    seconds.append(jnp.where(more[1], lists[0, 1, 1, 1], lists[0, 0, 1, 1]))
+    live = (True, True, more[0] | more[1])
+
+    def partner_of(l):
+        def partner(x, c):
+            if l == 0:
+                return resident[seconds[l], pl.ds(x, c)]
+            if l == 1:
+                return arrived[seconds[l], pl.ds(x, c)]
+            return jnp.where(
+                more[1],
+                arrived[seconds[l], pl.ds(x, c)].astype(F32),
+                resident[seconds[l], pl.ds(x, c)].astype(F32),
+            )
+
+        return partner
 
     def send(phase, src, dst, l, write):
         copies = []
         for o in range(1, parts):
-            write(lax.rem(me + o, parts))
-            c = remote(phase, src, dst, l, o)
+            to = lax.rem(me + o, parts)
+            write(to)
+            c = pltpu.make_async_remote_copy(
+                src_ref=src.at[l, to], dst_ref=dst.at[l, me],
+                send_sem=send_sem.at[phase, l, o], recv_sem=recv_sem.at[phase, l, o],
+                device_id=(block, to), device_id_type=MESH,
+            )
             c.start()
             copies.append(c)
         write(me)
@@ -311,77 +325,109 @@
         return copies
 
     flights = {}
-    for l in range(2):
+    for l in range(3):
         if l == 1:
             passing.wait()
-            saving = pltpu.make_async_copy(arrived, received, save_sem)
-            saving.start()
         peak = forward(
-            sz,
-            lambda x, c: own[firsts[l], pl.ds(x, c)],
-            lambda x, c: partners[l][seconds[l], pl.ds(x, c)],
-            wz, wy, t,
+            sz, lambda x, c: own[firsts[l], pl.ds(x, c)], partner_of(l), wz, wy, t
         )
         code = code_of(peak)
         flights[0, l] = send(
             0, out1, in1, l, lambda w: forward_words(sz, t, out1.at[l], w, code)
         )
-    for l in range(2):
+    for l in range(3):
         for c in flights[0, l]:
             c.wait()
         code = code_of(middle(sz, me, in1.at[l], wx, scales, u))
         flights[1, l] = send(
             1, out2, in2, l, lambda w: middle_words(sz, u, out2.at[l], w, code)
         )
-    for l in range(2):
+    bands = sz.bands
+    for l in range(3):
         for c in flights[1, l]:
             c.wait()
 
-        def add(x, v):
-            for band in range(sz.bands):
-                share = v * (firsts[l] == band).astype(F32)
+        def add(x, v, carried):
+            sums = []
+            for band in range(bands):
+                share = jnp.where((firsts[l] == band) & live[l], v, 0.0)
                 if l == 0:
-                    total[band, pl.ds(x, 2)] = share
+                    sooner = both & (lists[0, 0, 1, 0] == band)
+                    total[band, pl.ds(x, 2)] = share + jnp.where(
+                        sooner, early[pl.ds(x, 2)], 0.0
+                    )
+                elif l == 1:
+                    total[band, pl.ds(x, 2)] += share
                 else:
-                    total[band, pl.ds(x, 2)] += share
-
-        backward(
-            sz, in2.at[l], wz, wyi, scales, t,
-            lambda x, c: partners[l][seconds[l], pl.ds(x, c)], add,
-        )
-    saving.wait()
-
-
-def regular(sz, lists, own, resident, wz, wy, wx, wyi):
+                    sums.append(total[band, pl.ds(x, 2)] + share)
+                    result[band, pl.ds(x, 2)] = sums[-1].astype(BF16)
+            if l < 2:
+                return carried
+            carried = list(carried)
+            for i in range(bands):
+                mine = own[i, pl.ds(x, 2)].astype(F32)
+                for k in range(bands):
+                    product = (mine * sums[k]).reshape(-1, 8, sz.length)
+                    carried[i * bands + k] += jnp.sum(product, axis=0)
+            return tuple(carried)
+
+        start = 0
+        if l == 2:
+            start = (jnp.zeros((8, sz.length), F32),) * (bands * bands)
+        ended = backward(
+            sz, in2.at[l], wz, wyi, scales, t, partner_of(l), add, start
+        )
+    for i, v in enumerate(ended):
+        terms[me, i] = v
+    copies = []
+    for o in range(1, parts):
+        c = pltpu.make_async_remote_copy(
+            src_ref=terms.at[me], dst_ref=terms.at[me],
+            send_sem=term_send.at[o], recv_sem=term_recv.at[o],
+            device_id=(block, lax.rem(me + o, parts)), device_id_type=MESH,
+        )
+        c.start()
+        copies.append(c)
+    for c in copies:
+        c.wait()
+    inner[...] = sum(terms[g] for g in range(parts))
+
+
+def all_pairs(sz, lists, counts, own, resident, early, wz, wy, wx, wyi):
     n = sz.length
     vmem = pl.BlockSpec(memory_space=pltpu.VMEM)
-    coded = pltpu.VMEM((2,) + sz.coded(), I16)
+    smem = pl.BlockSpec(memory_space=pltpu.SMEM)
+    coded = pltpu.VMEM((3,) + sz.coded(), I16)
+    squared = sz.bands * sz.bands
     return pl.pallas_call(
-        functools.partial(regular_kernel, sz),
+        functools.partial(pairs_kernel, sz),
         out_shape=(
-            jax.ShapeDtypeStruct(own.shape, F32),
             jax.ShapeDtypeStruct(own.shape, BF16),
+            jax.ShapeDtypeStruct((squared, 8, n), F32),
         ),
-        in_specs=[pl.BlockSpec(memory_space=pltpu.SMEM)] + [vmem] * 6,
-        out_specs=(vmem, pl.BlockSpec(memory_space=pl.ANY)),
+        in_specs=[smem] * 2 + [vmem] * 7,
+        out_specs=(vmem, vmem),
         scratch_shapes=[
+            pltpu.VMEM(own.shape, F32),
             pltpu.VMEM(own.shape, BF16),
             pltpu.VMEM((n * sz.planes, n), F32),
             pltpu.VMEM((sz.rows, n, n), F32),
             pltpu.VMEM((n, n), F32),
             coded, coded, coded, coded,
-            pltpu.SemaphoreType.DMA((2, 2, sz.parts)),
-            pltpu.SemaphoreType.DMA((2, 2, sz.parts)),
+            pltpu.VMEM((sz.parts, squared, 8, n), F32),
+            pltpu.SemaphoreType.DMA((2, 3, sz.parts)),
+            pltpu.SemaphoreType.DMA((2, 3, sz.parts)),
             pltpu.SemaphoreType.DMA,
             pltpu.SemaphoreType.DMA,
-            pltpu.SemaphoreType.DMA((2, 2)),
-            pltpu.SemaphoreType.DMA,
+            pltpu.SemaphoreType.DMA((2, 3)),
+            pltpu.SemaphoreType.DMA((sz.parts,)),
+            pltpu.SemaphoreType.DMA((sz.parts,)),
         ],
         compiler_params=pltpu.CompilerParams(
             collective_id=0, has_side_effects=True, vmem_limit_bytes=LIMIT
         ),
-        name="regular_pairs",
-    )(lists, own, resident, wz, wy, wx, wyi)
+        name="all_pairs",
+    )(lists, counts, own, resident, early, wz, wy, wx, wyi)
 
 
 def extra_forward(sz, own, partner, wz, wy):
@@ -425,8 +471,9 @@
     n = sz.length
 
     def kernel(coded_ref, partner_ref, wz_ref, wyi_ref, out, scales, t):
-        def add(x, v):
+        def add(x, v, carried):
             out[pl.ds(x, 2)] = v
+            return carried
 
         backward(
             sz, coded_ref, wz_ref, wyi_ref, scales, t,
@@ -442,67 +489,28 @@
     )(coded, partner, wz, wyi)
 
 
-def finish(sz, own, total):
-    def kernel(own_ref, total_ref, out, products):
-        t = pl.program_id(0)
-
-        @pl.when(t == 0)
-        def _():
-            products[...] = jnp.zeros_like(products)
-
-        out[...] = total_ref[...].astype(BF16)
-        for i in range(sz.bands):
-            for k in range(sz.bands):
-                v = own_ref[i].astype(F32) * total_ref[k]
-                products[i, k] += jnp.sum(v.reshape(-1, 8, sz.length), axis=0)
-
-    step = 4
-    spec = pl.BlockSpec(
-        (sz.bands, step, sz.length, sz.length), lambda t: (0, t, 0, 0)
-    )
-    shape = (sz.bands, sz.bands, 8, sz.length)
-    return pl.pallas_call(
-        kernel,
-        grid=(sz.planes // step,),
-        in_specs=[spec, spec],
-        out_specs=(spec, pl.BlockSpec(shape, lambda t: (0, 0, 0, 0))),
-        out_shape=(
-            jax.ShapeDtypeStruct(own.shape, BF16),
-            jax.ShapeDtypeStruct(shape, F32),
-        ),
-        compiler_params=pltpu.CompilerParams(vmem_limit_bytes=LIMIT),
-        name="finish",
-    )(own, total)
-
-
 def on_device(own, resident, pair_lists, pair_counts):
     bands, planes, length, _ = own.shape
     sz = Sizes(bands, planes, length)
     wz, wy, wx, wyi = tables(length, sz.parts)
-    total, received = regular(sz, pair_lists, own, resident, wz, wy, wx, wyi)
-    extras = pair_counts[0] - 1
-
-    def one_pair(step, running):
-        l = (step >= extras[0]).astype(jnp.int32)
-        slot = 1 + step - l * extras[0]
-        row = pair_lists[0, l, slot]
+
+    def one_pair(_, term):
+        row = pair_lists[0, 0, 1]
         own_band = lax.dynamic_index_in_dim(own, row[0], 0, keepdims=False)
-        partner = jnp.where(
-            l == 0,
-            lax.dynamic_index_in_dim(resident, row[1], 0, keepdims=False),
-            lax.dynamic_index_in_dim(received, row[1], 0, keepdims=False),
-        )
+        partner = lax.dynamic_index_in_dim(resident, row[1], 0, keepdims=False)
         coded = extra_forward(sz, own_band, partner, wz, wy)
         coded = lax.all_to_all(coded, "grid", split_axis=0, concat_axis=0, tiled=True)
         coded = extra_middle(sz, coded, wx)
         coded = lax.all_to_all(coded, "grid", split_axis=0, concat_axis=0, tiled=True)
-        term = extra_backward(sz, coded, partner, wz, wyi)
-        old = lax.dynamic_index_in_dim(running, row[0], 0, keepdims=False)
-        return lax.dynamic_update_index_in_dim(running, old + term, row[0], 0)
-
-    total = lax.fori_loop(0, extras[0] + extras[1], one_pair, total)
-    rounded, products = finish(sz, own, total)
-    return rounded, lax.psum(jnp.sum(products, axis=(2, 3)), "grid")
+        return term + extra_backward(sz, coded, partner, wz, wyi)
+
+    ahead = (pair_counts[0, 0] - 1) * (pair_counts[0, 1] - 1)
+    early = jnp.zeros(own.shape[1:], F32)
+    early = lax.fori_loop(0, ahead, one_pair, early)
+    rounded, products = all_pairs(
+        sz, pair_lists, pair_counts, own, resident, early, wz, wy, wx, wyi
+    )
+    return rounded, jnp.sum(products, axis=(1, 2)).reshape(bands, bands)
 
 
 def solution(mesh):

time: 229 us -> 277 us (1.21)
  Pallas kernels: 152 us -> 196 us
  waiting for transfers between devices: 15.9 us -> 25.1 us
  other arithmetic: 6.87 us -> 0.83 us
  blocking collectives: 37.6 us -> 32.8 us
  loops' own time: 4.02 us -> 0.01 us
  between operations: 1.96 us -> 5.94 us
  local copies, waits for them, and re-layouts: 6.61 us -> 10.2 us
    pallas_call x2 -> x1, Pallas kernels: 126 us -> 169 us  [all_pairs(): pl.pallas_call(functools.partial(pairs_kernel, sz), out_shape=(jax.ShapeD...]
    psum x1 -> x0, blocking collectives: 10.4 us -> none  [on_device(): return (rounded, lax.psum(jnp.sum(products, axis=(2, 3)), 'grid'))]
    all_to_all x1, waiting for transfers between devices: 15.9 us -> 25.1 us  [one_pair(): lax.all_to_all(coded, 'grid', split_axis=0, concat_axis=0, tiled=True)]
    all_to_all x1, blocking collectives: 27.3 us -> 32.8 us  [one_pair(): lax.all_to_all(coded, 'grid', split_axis=0, concat_axis=0, tiled=True)]
    unnamed x6 -> x5, local copies, waits for them, and re-layouts: 0.02 us -> 4.17 us
    another operation x1, loops' own time: 4.02 us -> 0.01 us  [on_device(): early = lax.fori_loop(0, ahead, one_pair, early)]
    select_n x1 -> x0, other arithmetic: 3.44 us -> none  [one_pair(): jnp.where(l == 0, lax.dynamic_index_in_dim(resident, row[1], 0, keepdims=...]
    squeeze x0 -> x1, local copies, waits for them, and re-layouts: none -> 3.13 us  [one_pair(): partner = lax.dynamic_index_in_dim(resident, row[1], 0, keepdims=False)]
  transfers between devices with their start and end apart: 1 -> 1, of which waited for: 1 -> 1; matrix products, arithmetic and copies ran while one was open for 1% -> 0% of each run, Pallas kernels for 0% -> 0%
where the time goes in v1:
time: 277 us; the launch traced here: 274 us
  Pallas kernels  196 us (71%)
  blocking collectives  32.8 us (12%)
  waiting for transfers between devices  25.1 us (9%)
  local copies, waits for them, and re-layouts  10.2 us (4%)
  between operations  5.94 us (2%)
  starting transfers between devices  3.53 us (1%)
    pallas_call x1, Pallas kernels, all_pairs(): pl.pallas_call(functools.partial(pairs_kernel, sz), out_shape=(jax.ShapeD...  169 us
    all_to_all x1, blocking collectives, one_pair(): lax.all_to_all(coded, 'grid', split_axis=0, concat_axis=0, tiled=True)  32.8 us
    all_to_all x1, waiting for transfers between devices, one_pair(): lax.all_to_all(coded, 'grid', split_axis=0, concat_axis=0, tiled=True)  25.1 us
    pallas_call x1, Pallas kernels, extra_middle(): pl.pallas_call(kernel, out_shape=jax.ShapeDtypeStruct(sz.coded(), I16), s...  9.73 us
    pallas_call x1, Pallas kernels, extra_backward(): pl.pallas_call(kernel, out_shape=jax.ShapeDtypeStruct((sz.planes, n, n),...  9.39 us
    pallas_call x1, Pallas kernels, extra_forward(): pl.pallas_call(kernel, out_shape=jax.ShapeDtypeStruct(sz.coded(), I16), s...  7.81 us
  transfers between devices with their start and end apart: 1, of which 1 were waited for; matrix products, arithmetic and copies ran while one was open for 0% of the time, Pallas kernels for 0%

profile of v1, /device:TPU:6, one launch (start us, length us, event | category | flops | bytes accessed | tf_op | source)
XLA Modules:
  0.0 274.5 jit_solution(17128563814703336613)
XLA Ops:
  0.6 1.3 fusion
  6.0 3.1 %dynamic-slice_bitcast_fusion = (bf16[32,128,128]{2,1,0:T(8,128)(2,1)}, bf16[32,128,128]{2,1,0:T(8,128)(2,1)}) fusion(bf16[2,32,128,128]{3,2,1,0:T(8,128)(2,1)} %resident.1, s32[]{:T(128)S(6)} %select_n.12, bf16[2,32,128,128]{3,2,1,0:T(8,128)(2,1)} %own.1, s32[]{:T(128)S(6)} %select_n.11), kind=kLoop, calls=%fused_computation | loop fusion | bytes 4194312 | tf_op jit(solution)/shard_map/while/body/jit(dynamic_index_in_dim)/squeeze | solution.py:500
  9.1 7.8 %extra_forward.3 = s16[4,35,32,128]{3,2,1,0:T(8,128)(2,1)} custom-call(bf16[32,128,128]{2,1,0:T(8,128)(2,1)} %get-tuple-element.125.own_ref, bf16[32,128,128]{2,1,0:T(8,128)(2,1)} %get-tuple-element.124.partner_ref, bf16[256,256]{1,0:T(8,128)(2,1)} %constant.35.clone.wz_ref.wz, bf16[256,256]{1,0:T(8,128)(2,1)} %constant.36.clone.wy_ref.wy), custom_call_target="tpu_custom_call" | custom-call | tf_op jit(solution)/shard_map/while/body/extra_forward/pallas_call | solution.py:443
  16.9 32.8 %all_to_all.10.coded_ref = s16[4,35,32,128]{3,2,1,0:T(8,128)(2,1)} all-to-all(s16[4,35,32,128]{3,2,1,0:T(8,128)(2,1)} %extra_forward.3), channel_id=1, replica_groups=mesh['band'=8,'grid'=4] {'grid'}, dimensions={0} | all-to-all | bytes 2293760 | tf_op jit(solution)/shard_map/while/body/all_to_all | solution.py:502
  49.7 0.0 copy-start.1
  49.7 9.7 %extra_middle.3 = s16[4,35,32,128]{3,2,1,0:T(8,128)(2,1)} custom-call(s16[4,35,32,128]{3,2,1,0:T(8,128)(2,1)} %all_to_all.10.coded_ref, bf16[256,256]{1,0:T(8,128)(2,1)} %constant.37.clone.wx_ref.wx), custom_call_target="tpu_custom_call" | custom-call | tf_op jit(solution)/shard_map/while/body/extra_middle/pallas_call | solution.py:461
  59.5 3.5 %all-to-all-start.1 = ((s16[4,35,32,128]{3,2,1,0:T(8,128)(2,1)}), s16[4,35,32,128]{3,2,1,0:T(8,128)(2,1)S(1)}, u32[]{:S(2)}, u32[]{:S(2)}) async-start(s16[4,35,32,128]{3,2,1,0:T(8,128)(2,1)} %extra_middle.3), calls=%async_computation.1 | async-start | bytes 2293760 | tf_op jit(solution)/shard_map/while/body/all_to_all | solution.py:504
  63.0 0.0 copy-done.1
  63.0 0.7 fusion.1
  64.9 25.1 %all-to-all-done.1.coded_ref = s16[4,35,32,128]{3,2,1,0:T(8,128)(2,1)S(1)} async-done(((s16[4,35,32,128]{3,2,1,0:T(8,128)(2,1)}), s16[4,35,32,128]{3,2,1,0:T(8,128)(2,1)S(1)}, u32[]{:S(2)}, u32[]{:S(2)}) %all-to-all-start.1) | async-done | bytes 1146912 | tf_op jit(solution)/shard_map/while/body/all_to_all | solution.py:504
  90.0 0.0 copy-start
  90.0 1.0 copy-done
  91.0 9.4 %extra_backward.3 = f32[32,128,128]{2,1,0:T(8,128)} custom-call(s16[4,35,32,128]{3,2,1,0:T(8,128)(2,1)} %copy-done, bf16[32,128,128]{2,1,0:T(8,128)(2,1)} %get-tuple-element.124.partner_ref, bf16[256,256]{1,0:T(8,128)(2,1)} %constant.35.clone.wz_ref.wz, bf16[256,256]{1,0:T(8,128)(2,1)} %constant.38.clone.wyi_ref.wyi), custom_call_target="tpu_custom_call" | custom-call | tf_op jit(solution)/shard_map/while/body/extra_backward/pallas_call | solution.py:483
  100.4 0.2 broadcast_in_dim.3
  100.7 169.2 %all_pairs.1 = (bf16[2,32,128,128]{3,2,1,0:T(8,128)(2,1)}, f32[4,8,128]{2,1,0:T(8,128)}) custom-call(s32[1,2,2,2]{3,2,1,0:T(2,128)} %lists.1, s32[1,2]{1,0:T(1,128)} %counts.1, bf16[2,32,128,128]{3,2,1,0:T(8,128)(2,1)} %own.1, bf16[2,32,128,128]{3,2,1,0:T(8,128)(2,1)} %resident.1, f32[32,128,128]{2,1,0:T(8,128)S(1)} %get-tuple-element.109.early, ...), custom_call_target="tpu_custom_call" | custom-call | tf_op jit(solution)/shard_map/all_pairs/pallas_call | solution.py:402
  269.8 0.8 reduce_sum.9
  270.7 0.6 reshape.16
  271.3 3.2 %copy.19 = bf16[2,32,128,128]{3,2,1,0:T(8,128)(2,1)} copy(bf16[2,32,128,128]{3,2,1,0:T(8,128)(2,1)} %get-tuple-element.169) | data formatting | bytes 4194304
  (1 shorter events, 0.0 us)
Async XLA Ops:
  49.7 13.3 %copy-start.1 = (s32[1,2]{1,0:T(1,128)S(1)}, s32[1,2]{1,0:T(1,128)}, u32[]{:S(2)}) copy-start(s32[1,2]{1,0:T(1,128)} %counts.1) | copy-start | bytes 28
  59.5 30.5 %all-to-all-start.1 = ((s16[4,35,32,128]{3,2,1,0:T(8,128)(2,1)}), s16[4,35,32,128]{3,2,1,0:T(8,128)(2,1)S(1)}, u32[]{:S(2)}, u32[]{:S(2)}) async-start(s16[4,35,32,128]{3,2,1,0:T(8,128)(2,1)} %extra_middle.3), calls=%async_computation.1 | async-start | bytes 2293760 | tf_op jit(solution)/shard_map/while/body/all_to_all | solution.py:504
  90.0 1.0 copy-start
